TPU v7x, 256 devices: a whole 4x4x8 slice. The times are simulated.
256 devices in a mesh: dp: 8 (over z_hi, y), expert: 16 (over z_lo, x), head: 2 (over core).
Axes of the slice: x: 4, y: 4, z: 8 (z_hi: 2, z_lo: 4; z = z_hi * 4 + z_lo), core: 2. Of those that a mesh axis runs over, the one named last changes fastest.
Arguments:
- prev_rows: bfloat16 [16384, 5120], P(('dp', 'expert'), 'head'), may hold values from -6 to 6
- current: bfloat16 [16384, 5120], P(('dp', 'expert'), 'head'), may hold values from -6 to 6
- expert_ids: int32 [16384, 6], P(('dp', 'expert')), may hold values from 0 to 15, all different within a row; in each aligned block of 128 rows (0 to 127, 128 to 255, ...) at most 72 rows name the same one
- gate_weights: float32 [16384, 6], P(('dp', 'expert')), may hold values from 0.1 to 1
- w_in: bfloat16 [16, 2, 768, 5120], P('expert', None, 'dp', 'head'), may hold values from -0.078125 to 0.078125
- w_down: bfloat16 [16, 768, 5120], P('expert', 'dp', 'head'), may hold values from -0.21875 to 0.21875
Outputs:
- blended: bfloat16 [16384, 5120], P(('dp', 'expert'), 'head')
Inputs may be any that keep to these rules, and one draw needn't show every extreme that they name: `expert_ids`: each row names 6 different experts. Within the rows of one index pair of dp and expert (128 aligned rows) no expert is named by more than 72 rows, a bound that some expert reaches in some of these blocks.
All inputs are finite; a program needn't handle non-finite values.
Results may differ from a plain program's by a relative error of at most 0.0052.
Values may be sent and summed in bfloat16 or wider, within the bound.
No kernel may reach another device: no remote copies, remote signals or barrier semaphores. Data moves between devices by JAX's collectives and lax.ppermute only.
A program may use at most 128 MiB of HBM per device.

v0:
```python
import jax
import jax.numpy as jnp
from jax import lax
from jax.sharding import PartitionSpec as P


def local(prev_rows, current, expert_ids, gate_weights, w_in, w_down):
    row_count, fanout = expert_ids.shape
    experts = lax.axis_size("expert")
    capacity = min(row_count, 3 * fanout * row_count // (2 * experts))
    chosen = expert_ids.reshape(-1)
    matches = (chosen[:, None] == jnp.arange(experts, dtype=jnp.int32)[None, :]).astype(jnp.int32)
    before = jnp.cumsum(matches, axis=0) - matches
    position = jnp.sum(before * matches, axis=1)
    slot_index = chosen * capacity + position
    owners = jnp.arange(row_count * fanout, dtype=jnp.int32) // fanout
    source = jnp.zeros((experts * capacity,), jnp.int32).at[slot_index].set(owners)
    filled = jnp.zeros((experts * capacity,), jnp.bool_).at[slot_index].set(True)
    outgoing = jnp.where(filled[:, None], prev_rows[source], jnp.zeros((), prev_rows.dtype))
    incoming = lax.all_to_all(outgoing, "expert", split_axis=0, concat_axis=0, tiled=True)
    partial_value = jnp.einsum(
        "rd,gfd->rgf",
        incoming,
        lax.all_gather(w_in, "dp", axis=2, tiled=True)[0],
        preferred_element_type=jnp.float32,
    )
    summed = lax.psum(partial_value, "head")
    hidden = (jax.nn.silu(summed[:, 0]) * summed[:, 1]).astype(jnp.bfloat16)
    expert_out = jnp.dot(
        hidden,
        lax.all_gather(w_down, "dp", axis=1, tiled=True)[0],
        preferred_element_type=jnp.float32,
    )
    returned = lax.all_to_all(
        expert_out.astype(jnp.bfloat16), "expert", split_axis=0, concat_axis=0, tiled=True
    )
    picked = returned[slot_index].reshape(row_count, fanout, returned.shape[1])
    weighted = jnp.sum(gate_weights[:, :, None] * picked.astype(jnp.float32), axis=1)
    blended = current.astype(jnp.float32) + weighted
    return blended.astype(jnp.bfloat16)


def solution(mesh):
    placed = (
        P(("dp", "expert"), "head"),
        P(("dp", "expert"), "head"),
        P(("dp", "expert"), None),
        P(("dp", "expert"), None),
        P("expert", None, "dp", "head"),
        P("expert", "dp", "head"),
    )
    return jax.shard_map(
        local, mesh=mesh, in_specs=placed, out_specs=P(("dp", "expert"), "head"), check_vma=False
    )
```

profile of v0, /device:TPU:64, one launch (start us, length us, event | category | flops | bytes accessed | tf_op | source)
XLA Modules:
  0.0 574.0 jit_solution(3616293740309351367)
XLA Ops:
  6.5 0.0 copy-start
  6.5 0.0 all-gather.3.cloned.1.call-start
  6.5 0.7 all-gather.3.cloned.1.call-update
  7.3 0.8 copy.10
  8.1 0.1 eq.29
  8.2 0.1 eq.25
  8.3 1.7 reduce-window.6
  10.1 0.3 slice_reduce_fusion
  10.3 0.7 broadcast_multiply_fusion
  11.0 0.1 copy.9
  11.2 0.1 mul.39
  11.3 0.1 fusion.8
  11.4 3.4 scatter_custom_fusion.1
  14.8 3.4 scatter_custom_fusion
  18.2 0.1 broadcast_in_dim.31
  18.3 0.0 copy-done
  18.4 6.4 %gather_fusion = bf16[1152,2560]{1,0:T(8,128)(2,1)} fusion(bf16[128,2560]{1,0:T(8,128)(2,1)S(1)} %copy-done, s32[2048]{0:T(1024)S(1)} %pad_clamp_fusion), kind=kCustom, calls=%fused_computation | custom fusion | bytes 11801088 | tf_op jit(solution)/shard_map/gather | solution.py:19
  24.7 6.3 %broadcast_select_fusion = bf16[16,72,2560]{2,1,0:T(8,128)(2,1)} fusion(bf16[16,72,2560]{2,1,0:T(8,128)(2,1)} %bitcast.36, pred[16,72]{1,0:T(8,128)(4,1)S(1)} %broadcast_in_dim.31), kind=kLoop, calls=%fused_computation.8 | loop fusion | flops 2949120 | bytes 11797632 | tf_op jit(solution)/shard_map/jit(_where)/select_n | solution.py:19
  31.0 7.9 %all-to-all-start = ((bf16[16,72,2560]{2,1,0:T(8,128)(2,1)}), bf16[16,72,2560]{2,1,0:T(8,128)(2,1)}, u32[]{:S(2)}, u32[]{:S(2)}) async-start(bf16[16,72,2560]{2,1,0:T(8,128)(2,1)} %broadcast_select_fusion), calls=%async_computation | async-start | bytes 11796480 | tf_op jit(solution)/shard_map/all_to_all | solution.py:20
  38.9 0.0 all-gather.5.cloned.1.call-start
  38.9 0.7 all-gather.5.cloned.1.call-update
  39.7 0.2 all-reduce.2.cloned.1.call-start
  39.9 232.3 %all-to-all-done = bf16[16,72,2560]{2,1,0:T(8,128)(2,1)} async-done(((bf16[16,72,2560]{2,1,0:T(8,128)(2,1)}), bf16[16,72,2560]{2,1,0:T(8,128)(2,1)}, u32[]{:S(2)}, u32[]{:S(2)}) %all-to-all-start) | async-done | bytes 5898272 | tf_op jit(solution)/shard_map/all_to_all | solution.py:20
  272.1 0.0 all-gather.3.cloned.1.call-done
  272.1 15.4 %fusion = f32[1152,2,768]{2,0,1:T(8,128)} fusion(bf16[1152,2560,1]{1,0,2:T(8,128)(2,1)} %bitcast.3, bf16[1,2,768,2560]{3,2,1,0:T(8,128)(2,1)} %all-gather.3.cloned.1.call-done), kind=kOutput, calls=%fused_computation.6 | convolution fusion | flops 9059696640 | bytes 20840448 | tf_op jit(solution)/shard_map/rd,gfd->rgf/dot_general | solution.py:21
  287.5 0.0 all-reduce.2.cloned.1.call-update
  287.5 58.0 %all-gather.5.cloned.1.call-done = bf16[1,768,2560]{2,1,0:T(8,128)(2,1)} async-done(((bf16[1,96,2560]{2,1,0:T(8,128)(2,1)}), bf16[1,768,2560]{2,1,0:T(8,128)(2,1)}) %all-gather.5.cloned.1.call-update) | async-done | bytes 3932176 | tf_op jit(solution)/shard_map/all_gather | solution.py:31
  345.5 43.9 %all-reduce.2.cloned.1.call-done = f32[1152,2,768]{2,0,1:T(8,128)} async-done(((f32[1152,2,768]{2,0,1:T(8,128)}), f32[1152,2,768]{2,0,1:T(8,128)}) %all-reduce.2.cloned.1.call-update) | async-done | bytes 7077904 | tf_op jit(solution)/shard_map/psum | solution.py:27
  389.4 11.5 %convolution_convert_fusion = bf16[1152,2560]{1,0:T(8,128)(2,1)} fusion(bf16[1,768,2560]{2,1,0:T(8,128)(2,1)} %all-gather.5.cloned.1.call-done, f32[1152,2,768]{2,0,1:T(8,128)} %all-reduce.2.cloned.1.call-done), kind=kOutput, calls=%fused_computation.4 | convolution fusion | flops 4538105856 | bytes 16908288 | tf_op jit(solution)/shard_map/dot_general | solution.py:29
  400.9 0.0 copy-start.3
  400.9 7.8 %all-to-all-start.1 = ((bf16[16,72,2560]{2,1,0:T(8,128)(2,1)}), bf16[16,72,2560]{2,1,0:T(8,128)(2,1)}, u32[]{:S(2)}, u32[]{:S(2)}) async-start(bf16[16,72,2560]{2,1,0:T(8,128)(2,1)} %bitcast.37), calls=%async_computation.1 | async-start | bytes 11796480 | tf_op jit(solution)/shard_map/all_to_all | solution.py:34
  408.6 0.0 copy-done.3
  408.6 0.1 copy.8
  408.8 130.2 %all-to-all-done.1 = bf16[16,72,2560]{2,1,0:T(8,128)(2,1)} async-done(((bf16[16,72,2560]{2,1,0:T(8,128)(2,1)}), bf16[16,72,2560]{2,1,0:T(8,128)(2,1)}, u32[]{:S(2)}, u32[]{:S(2)}) %all-to-all-start.1) | async-done | bytes 5898272 | tf_op jit(solution)/shard_map/all_to_all | solution.py:34
  538.9 11.8 %gather_fusion.1 = bf16[768,2560]{1,0:T(8,128)(2,1)} fusion(bf16[1152,2560]{1,0:T(8,128)(2,1)} %bitcast.8, s32[1024]{0:T(1024)S(1)} %pad_clamp_fusion.1), kind=kCustom, calls=%fused_computation.1 | custom fusion | bytes 7867392 | tf_op jit(solution)/shard_map/gather | solution.py:37
  550.7 0.0 copy-start.1
  550.7 7.8 %reshape.63 = f32[128,6,2560]{2,1,0:T(8,128)} reshape(bf16[768,2560]{1,0:T(8,128)(2,1)} %gather_fusion.1) | data formatting | bytes 11796480 | tf_op jit(solution)/shard_map/convert_element_type | solution.py:38
  558.5 0.0 copy-start.2
  558.5 8.0 %multiply_reduce_fusion = f32[128,2560]{1,0:T(8,128)S(1)} fusion(f32[128,6,2560]{2,1,0:T(8,128)} %reshape.63, f32[128,6]{1,0:T(8,128)S(1)} %copy.8), kind=kLoop, calls=%fused_computation.5 | loop fusion | flops 3604480 | bytes 9178112 | tf_op jit(solution)/shard_map/reduce_sum | solution.py:38
  566.5 0.0 copy-done.2
  566.5 0.9 add_convert_fusion
  567.4 0.0 copy-done.1
  (8 shorter events, 0.1 us)
Async XLA Ops:
  6.5 11.8 %copy-start = (bf16[128,2560]{1,0:T(8,128)(2,1)S(1)}, bf16[128,2560]{1,0:T(8,128)(2,1)}, u32[]{:S(2)}) copy-start(bf16[128,2560]{1,0:T(8,128)(2,1)} %param.6) | copy-start | bytes 1966084
  6.5 265.6 %all-gather.3.cloned.1.call-start = ((), (), s32[]{:S(2)}) async-start(), calls=%async_computation.2 | async-start | bytes 8847360 | tf_op jit(solution)/shard_map/all_gather | solution.py:24
  31.0 241.1 %all-to-all-start = ((bf16[16,72,2560]{2,1,0:T(8,128)(2,1)}), bf16[16,72,2560]{2,1,0:T(8,128)(2,1)}, u32[]{:S(2)}, u32[]{:S(2)}) async-start(bf16[16,72,2560]{2,1,0:T(8,128)(2,1)} %broadcast_select_fusion), calls=%async_computation | async-start | bytes 11796480 | tf_op jit(solution)/shard_map/all_to_all | solution.py:20
  38.9 306.6 %all-gather.5.cloned.1.call-start = ((), (), s32[]{:S(2)}) async-start(), calls=%async_computation.4 | async-start | bytes 4423680 | tf_op jit(solution)/shard_map/all_gather | solution.py:31
  39.7 349.7 %all-reduce.2.cloned.1.call-start = ((), (), s32[]{:S(2)}) async-start(), calls=%async_computation.3 | async-start | bytes 14155776 | tf_op jit(solution)/shard_map/psum | solution.py:27
  400.9 7.8 %copy-start.3 = (f32[128,6]{0,1:T(8,128)S(1)}, f32[128,6]{0,1:T(8,128)}, u32[]{:S(2)}) copy-start(f32[128,6]{0,1:T(8,128)} %param.9) | copy-start | bytes 9220
  400.9 138.1 %all-to-all-start.1 = ((bf16[16,72,2560]{2,1,0:T(8,128)(2,1)}), bf16[16,72,2560]{2,1,0:T(8,128)(2,1)}, u32[]{:S(2)}, u32[]{:S(2)}) async-start(bf16[16,72,2560]{2,1,0:T(8,128)(2,1)} %bitcast.37), calls=%async_computation.1 | async-start | bytes 11796480 | tf_op jit(solution)/shard_map/all_to_all | solution.py:34
  550.7 16.7 %copy-start.1 = (bf16[128,2560]{1,0:T(8,128)(2,1)S(1)}, bf16[128,2560]{1,0:T(8,128)(2,1)}, u32[]{:S(2)}) copy-start(bf16[128,2560]{1,0:T(8,128)(2,1)} %param.6) | copy-start | bytes 1966084
  558.5 8.0 %copy-start.2 = (bf16[128,2560]{1,0:T(8,128)(2,1)S(1)}, bf16[128,2560]{1,0:T(8,128)(2,1)}, u32[]{:S(2)}) copy-start(bf16[128,2560]{1,0:T(8,128)(2,1)} %param.7) | copy-start | bytes 1966084
Sparse Core Ops, SparseCore 0:
  9.9 190.8 all-gather.2
  203.4 142.0 all-gather.4
  348.2 41.0 all-reduce.1
where the time goes:
time: 575 us; the launch traced here: 574 us
  waiting for transfers between devices  466 us (81%)
  local copies, waits for them, and re-layouts  34.5 us (6%)
  matrix products  26.9 us (5%)
  other arithmetic  17.8 us (3%)
  starting transfers between devices  15.9 us (3%)
  between operations  13.2 us (2%)
    all_to_all x1, waiting for transfers between devices, local(): lax.all_to_all(outgoing, 'expert', split_axis=0, concat_axis=0, tiled=True)  232 us
    all_to_all x1, waiting for transfers between devices, local(): lax.all_to_all(expert_out.astype(jnp.bfloat16), 'expert', split_axis=0, c...  130 us
    all_gather x1, waiting for transfers between devices, local(): lax.all_gather(w_down, 'dp', axis=1, tiled=True)[0]  58 us
    psum x1, waiting for transfers between devices, local(): summed = lax.psum(partial_value, 'head')  43.9 us
    dot_general x1, matrix products, local(): jnp.einsum('rd,gfd->rgf', incoming, lax.all_gather(w_in, 'dp', axis=2, ti...  15.4 us
    gather x1, local copies, waits for them, and re-layouts, local(): picked = returned[slot_index].reshape(row_count, fanout, returned.shape[1])  11.8 us
    dot_general x1, matrix products, local(): jnp.dot(hidden, lax.all_gather(w_down, 'dp', axis=1, tiled=True)[0], pref...  11.5 us
  transfers between devices with their start and end apart: 5, of which 4 were waited for; matrix products, arithmetic and copies ran while one was open for 7% of the time, Pallas kernels for 0%

commit v1 on v0

v1 whole, which is shorter than its diff:
```python
import jax
import jax.numpy as jnp
from jax import lax
from jax.sharding import PartitionSpec as P

NX, NY, NZ, NLO = 4, 4, 8, 4
CAP = 72
BF = jnp.bfloat16
F32 = jnp.float32
AXES = ("dp", "expert")
XGROUPS = [[NX * i + j for j in range(NX)] for i in range(NLO)]
YGROUPS = [[NY * i + j for j in range(NY)] for i in range(NZ // NLO)]


def place(i):
    dp, ex = divmod(i, NLO * NX)
    zh, y = divmod(dp, NY)
    zl, x = divmod(ex, NX)
    return x, y, zh * NLO + zl


def index(x, y, z):
    z %= NZ
    return ((z // NLO) * NY + y % NY) * NLO * NX + (z % NLO) * NX + x % NX


def shift(v, dy=0, dz=0):
    pairs = []
    for i in range(NX * NY * NZ):
        x, y, z = place(i)
        pairs.append((i, index(x, y + dy, z + dz)))
    return lax.ppermute(v, AXES, pairs)


def skip(v, sign):
    pairs = []
    for i in range(NX * NY * NZ):
        x, y, z = place(i)
        pairs.append((i, index(x, y, z + 2 * sign * (1 if z % 2 == 0 else -1))))
    return lax.ppermute(v, AXES, pairs)


def swap_x(v):
    return lax.all_to_all(
        v, "expert", split_axis=0, concat_axis=0, tiled=True, axis_index_groups=XGROUPS
    )


def after(v, *others):
    return lax.optimization_barrier((v,) + others)[0]


def spread_y(v, axis):
    left = shift(v, dy=1)
    right = shift(v, dy=-1)
    half = v.shape[0] // 2
    far = jnp.concatenate([shift(left[:half], dy=1), shift(right[half:], dy=-1)], axis=0)
    return jnp.concatenate([v, left, right, far], axis=axis)


def route(ids, gates, first):
    count = ids.shape[0]
    experts = first + jnp.arange(NX, dtype=jnp.int32)
    hit = ids[:, None, :] == experts[None, :, None]
    member = jnp.any(hit, axis=2)
    weight = jnp.sum(jnp.where(hit, gates[:, None, :], 0.0), axis=2)
    row = lax.broadcasted_iota(jnp.int32, (count, count), 0)
    col = lax.broadcasted_iota(jnp.int32, (count, count), 1)
    position = jnp.dot((col < row).astype(BF), member.astype(BF), preferred_element_type=F32)
    slots = jnp.arange(CAP, dtype=jnp.int32).astype(F32)
    chosen = member[:, :, None] & (position[:, :, None] == slots[None, None, :])
    high = lax.reduce_precision(weight, 8, 7)
    low = weight - high
    pick = chosen.reshape(count, NX * CAP)
    spread = lambda w: jnp.where(chosen, w[:, :, None], 0.0).astype(BF).reshape(count, NX * CAP)
    return pick.astype(BF).T, spread(high), spread(low)


def local(prev_rows, current, expert_ids, gate_weights, w_in, w_down):
    fanout = expert_ids.shape[1]
    first = (lax.axis_index("expert") // NX) * NX
    w_in, w_down = w_in[0], w_down[0]

    small = jnp.concatenate([expert_ids.astype(F32), gate_weights], axis=1)
    smalls = [small, shift(small, dz=1), shift(small, dz=-1), skip(small, 1)]
    blocks = [prev_rows, shift(prev_rows, dz=1), shift(prev_rows, dz=-1), skip(prev_rows, 1)]
    routes = [route(s[:, :fanout].astype(jnp.int32), s[:, fanout:], first) for s in smalls]

    near_in = lax.all_gather(w_in, "dp", axis=1, tiled=True, axis_index_groups=YGROUPS)
    near_down = lax.all_gather(w_down, "dp", axis=0, tiled=True, axis_index_groups=YGROUPS)
    other_in = shift(after(w_in, blocks[1], blocks[2]), dz=NLO)
    other_down = shift(after(w_down, blocks[3]), dz=NLO)
    far_in = spread_y(other_in, 1)
    far_down = spread_y(other_down, 0)

    sent = [jnp.dot(r[0], b, preferred_element_type=F32).astype(BF) for r, b in zip(routes, blocks)]
    mine = swap_x(sent[0])
    rest = jnp.stack([s.reshape(NX, CAP, -1) for s in sent[1:]], axis=1).reshape(NX, 3 * CAP, -1)
    rest = swap_x(rest)
    rows = jnp.concatenate(
        [mine.reshape(NX, 1, CAP, -1), rest.reshape(NX, 3, CAP, -1)], axis=1
    ).reshape(NX * 4 * CAP, -1)

    def project(weights):
        value = lax.dot_general(
            rows,
            weights.reshape(-1, weights.shape[2]),
            (((1,), (1,)), ((), ())),
            preferred_element_type=F32,
        )
        other = lax.ppermute(value.astype(BF), "head", [(0, 1), (1, 0)])
        total = value + other.astype(F32)
        width = total.shape[1] // 2
        return (jax.nn.silu(total[:, :width]) * total[:, width:]).astype(BF)

    hidden_near = project(near_in).reshape(NX, 4, CAP, -1)
    hidden_far = project(far_in).reshape(NX, 4, CAP, -1)
    hidden = jnp.concatenate([hidden_near, hidden_far], axis=3)
    down = jnp.concatenate([near_down, far_down], axis=0)

    partials = [None] * 4
    for b in (3, 1, 2, 0):
        produced = jnp.dot(
            hidden[:, b].reshape(NX * CAP, -1), down, preferred_element_type=F32
        ).astype(BF)
        returned = swap_x(produced)
        _, high, low = routes[b]
        partials[b] = jnp.dot(high, returned, preferred_element_type=F32) + jnp.dot(
            low, returned, preferred_element_type=F32
        )
    total = current.astype(F32) + partials[0]
    total = total + skip(partials[3].astype(BF), -1).astype(F32)
    total = total + shift(partials[1].astype(BF), dz=-1).astype(F32)
    total = total + shift(partials[2].astype(BF), dz=1).astype(F32)
    return total.astype(BF)


def solution(mesh):
    placed = (
        P(("dp", "expert"), "head"),
        P(("dp", "expert"), "head"),
        P(("dp", "expert"), None),
        P(("dp", "expert"), None),
        P("expert", None, "dp", "head"),
        P("expert", "dp", "head"),
    )
    return jax.shard_map(
        local, mesh=mesh, in_specs=placed, out_specs=P(("dp", "expert"), "head"), check_vma=False
    )
```

time: 575 us -> 307 us (0.53)
  waiting for transfers between devices: 466 us -> 123 us
  starting transfers between devices: 15.9 us -> 82.9 us
  matrix products: 26.9 us -> 53 us
  local copies, waits for them, and re-layouts: 34.5 us -> 13.8 us
    all_to_all x2 -> x6, waiting for transfers between devices: 362 us -> 34.2 us  [swap_x(): lax.all_to_all(v, 'expert', split_axis=0, concat_axis=0, tiled=True, axis...]
    ppermute x0 -> x21, waiting for transfers between devices: none -> 88.3 us  [the longest x16 88.3 us: shift(): return lax.ppermute(v, AXES, pairs)]
    all_gather x2, waiting for transfers between devices: 58 us -> 0.01 us  [the longest x1 0.01 us: local(): lax.all_gather(w_down, 'dp', axis=0, tiled=True, axis_index_groups=YGROUPS)]
    ppermute x0 -> x21, starting transfers between devices: none -> 56.9 us  [the longest x16 28.5 us: shift(): return lax.ppermute(v, AXES, pairs)]
    psum x1 -> x0, waiting for transfers between devices: 43.9 us -> none  [local(): summed = lax.psum(partial_value, 'head')]
    dot_general x2 -> x22, matrix products: 26.9 us -> 53 us  [the longest x4 18.3 us: local(): jnp.dot(hidden[:, b].reshape(NX * CAP, -1), down, preferred_element_type=...]
    gather x2 -> x0, local copies, waits for them, and re-layouts: 18.1 us -> none  [the longest x1 11.8 us: local(): picked = returned[slot_index].reshape(row_count, fanout, returned.shape[1])]
    all_to_all x2 -> x6, starting transfers between devices: 15.7 us -> 26 us  [swap_x(): lax.all_to_all(v, 'expert', split_axis=0, concat_axis=0, tiled=True, axis...]
  transfers between devices with their start and end apart: 5 -> 29, of which waited for: 4 -> 12; matrix products, arithmetic and copies ran while one was open for 7% -> 24% of each run, Pallas kernels for 0% -> 0%
where the time goes in v1:
time: 307 us; the launch traced here: 303 us
  waiting for transfers between devices  123 us (40%)
  starting transfers between devices  82.9 us (27%)
  matrix products  53 us (17%)
  other arithmetic  16.3 us (5%)
  between operations  13.9 us (5%)
  local copies, waits for them, and re-layouts  13.8 us (4%)
    ppermute x16, waiting for transfers between devices, shift(): return lax.ppermute(v, AXES, pairs)  88.3 us
    all_to_all x6, waiting for transfers between devices, swap_x(): lax.all_to_all(v, 'expert', split_axis=0, concat_axis=0, tiled=True, axis...  34.2 us
    ppermute x16, starting transfers between devices, shift(): return lax.ppermute(v, AXES, pairs)  28.5 us
    ppermute x3, starting transfers between devices, skip(): return lax.ppermute(v, AXES, pairs)  27.8 us
    all_to_all x6, starting transfers between devices, swap_x(): lax.all_to_all(v, 'expert', split_axis=0, concat_axis=0, tiled=True, axis...  26 us
    dot_general x4, matrix products, local(): jnp.dot(hidden[:, b].reshape(NX * CAP, -1), down, preferred_element_type=...  18.3 us
    dot_general x2, matrix products, project(): lax.dot_general(rows, weights.reshape(-1, weights.shape[2]), (((1,), (1,)...  14.1 us
    dot_general x4, matrix products, local(): jnp.dot(high, returned, preferred_element_type=F32)  9.42 us
  transfers between devices with their start and end apart: 29, of which 12 were waited for; matrix products, arithmetic and copies ran while one was open for 24% of the time, Pallas kernels for 0%

profile of v1, /device:TPU:64, one launch (start us, length us, event | category | flops | bytes accessed | tf_op | source)
XLA Modules:
  0.0 303.2 jit_solution(8283208069272671381)
XLA Ops:
  8.7 1.9 collective-permute-start
  10.7 5.7 %collective-permute-start.4 = (f32[128,12]{0,1:T(8,128)S(1)}, f32[128,12]{0,1:T(8,128)S(1)}, u32[]{:S(2)}, u32[]{:S(2)}) collective-permute-start(f32[128,12]{0,1:T(8,128)S(1)} %pad_maximum_fusion.3), channel_id=1, source_target_pairs={{0,16},{2,18},{4,20},{6,22},{8,152},{10,154},{12,156},{14,158},{16... | collective-permute-start | bytes 18440 | tf_op jit(solution)/shard_map/ppermute | solution.py:40
  16.9 1.8 collective-permute-start.1
  21.4 12.9 %collective-permute-done.3 = bf16[128,2560]{1,0:T(8,128)(2,1)S(1)} collective-permute-done((bf16[128,2560]{1,0:T(8,128)(2,1)}, bf16[128,2560]{1,0:T(8,128)(2,1)S(1)}, u32[]{:S(2)}, u32[]{:S(2)}) %collective-permute-start.3) | collective-permute-done | bytes 655392 | tf_op jit(solution)/shard_map/ppermute | solution.py:32
  34.3 12.8 %collective-permute-done.1 = bf16[128,2560]{1,0:T(8,128)(2,1)S(1)} collective-permute-done((bf16[128,2560]{1,0:T(8,128)(2,1)}, bf16[128,2560]{1,0:T(8,128)(2,1)S(1)}, u32[]{:S(2)}, u32[]{:S(2)}) %collective-permute-start.1) | collective-permute-done | bytes 655392 | tf_op jit(solution)/shard_map/ppermute | solution.py:32
  47.1 2.5 collective-permute-start.7
  49.6 1.7 convolution_convert_fusion.7
  51.3 4.3 %all-to-all-start = ((bf16[4,72,2560]{2,1,0:T(8,128)(2,1)}), bf16[4,72,2560]{2,1,0:T(8,128)(2,1)S(1)}, u32[]{:S(2)}, u32[]{:S(2)}) async-start(bf16[4,72,2560]{2,1,0:T(8,128)(2,1)} %bitcast.2), calls=%async_computation | async-start | bytes 2949120 | tf_op jit(solution)/shard_map/all_to_all | solution.py:44
  55.6 3.4 %collective-permute-start.13 = (bf16[96,2560]{1,0:T(8,128)(2,1)}, bf16[96,2560]{1,0:T(8,128)(2,1)}, u32[]{:S(2)}, u32[]{:S(2)}) collective-permute-start(bf16[96,2560]{1,0:T(8,128)(2,1)} %bitcast.27), channel_id=1, source_target_pairs={{0,128},{2,130},{4,132},{6,134},{8,136},{10,138},{12,140},{14,142}... | collective-permute-start | bytes 1474568 | tf_op jit(solution)/shard_map/ppermute | solution.py:32
  59.1 1.7 convolution_convert_fusion.5
  63.0 24.9 %collective-permute-done.7 = bf16[2,96,2560]{2,1,0:T(8,128)(2,1)} collective-permute-done((bf16[2,96,2560]{2,1,0:T(8,128)(2,1)S(1)}, bf16[2,96,2560]{2,1,0:T(8,128)(2,1)}, u32[]{:S(2)}, u32[]{:S(2)}) %collective-permute-start.7) | collective-permute-done | bytes 983072 | tf_op jit(solution)/shard_map/ppermute | solution.py:32
  89.4 1.7 collective-permute-start.9
  91.1 2.3 pad_maximum_fusion.1
  93.4 4.9 %all-to-all-start.1 = ((bf16[4,216,2560]{2,1,0:T(8,128)(2,1)}), bf16[4,216,2560]{2,1,0:T(8,128)(2,1)}, u32[]{:S(2)}, u32[]{:S(2)}) async-start(bf16[4,216,2560]{2,1,0:T(8,128)(2,1)} %bitcast.122), calls=%async_computation.1 | async-start | bytes 8847360 | tf_op jit(solution)/shard_map/all_to_all | solution.py:44
  98.3 4.5 %collective-permute-done.13 = bf16[96,2560]{1,0:T(8,128)(2,1)} collective-permute-done((bf16[96,2560]{1,0:T(8,128)(2,1)}, bf16[96,2560]{1,0:T(8,128)(2,1)}, u32[]{:S(2)}, u32[]{:S(2)}) %collective-permute-start.13) | collective-permute-done | bytes 491552 | tf_op jit(solution)/shard_map/ppermute | solution.py:32
  104.4 1.7 collective-permute-start.15
  106.0 19.5 %collective-permute-done.14 = bf16[96,2560]{1,0:T(8,128)(2,1)S(1)} collective-permute-done((bf16[96,2560]{1,0:T(8,128)(2,1)}, bf16[96,2560]{1,0:T(8,128)(2,1)S(1)}, u32[]{:S(2)}, u32[]{:S(2)}) %collective-permute-start.14) | collective-permute-done | bytes 491552 | tf_op jit(solution)/shard_map/ppermute | solution.py:32
  127.1 3.2 %collective-permute-start.17 = (bf16[48,2560]{1,0:T(8,128)(2,1)}, bf16[48,2560]{1,0:T(8,128)(2,1)}, u32[]{:S(2)}, u32[]{:S(2)}) collective-permute-start(bf16[48,2560]{1,0:T(8,128)(2,1)} %slice.84), channel_id=1, source_target_pairs={{0,96},{2,98},{4,100},{6,102},{8,104},{10,106},{12,108},{14,110},{... | collective-permute-start | bytes 737288 | tf_op jit(solution)/shard_map/ppermute | solution.py:32
  131.9 3.2 %collective-permute-start.11 = (bf16[1,96,2560]{2,1,0:T(8,128)(2,1)}, bf16[1,96,2560]{2,1,0:T(8,128)(2,1)}, u32[]{:S(2)}, u32[]{:S(2)}) collective-permute-start(bf16[1,96,2560]{2,1,0:T(8,128)(2,1)} %slice.78), channel_id=1, source_target_pairs={{0,96},{2,98},{4,100},{6,102},{8,104},{10,106},{12,108},{14,110},{... | collective-permute-start | bytes 1474568 | tf_op jit(solution)/shard_map/ppermute | solution.py:32
  135.2 3.0 bitcast_dynamic-update-slice_fusion
  138.2 1.9 constant_dynamic-update-slice_fusion.4
  141.7 3.5 %collective-permute-done.10 = bf16[1,96,2560]{2,1,0:T(8,128)(2,1)} collective-permute-done((bf16[1,96,2560]{2,1,0:T(8,128)(2,1)}, bf16[1,96,2560]{2,1,0:T(8,128)(2,1)}, u32[]{:S(2)}, u32[]{:S(2)}) %collective-permute-start.10) | collective-permute-done | bytes 491552 | tf_op jit(solution)/shard_map/ppermute | solution.py:32
  145.3 3.3 %maximum_maximum_fusion = bf16[2,384,2560]{2,1,0:T(8,128)(2,1)} fusion(bf16[1,96,2560]{2,1,0:T(8,128)(2,1)} %collective-permute-done.11, bf16[1,96,2560]{2,1,0:T(8,128)(2,1)} %collective-permute-done.10, bf16[2,96,2560]{2,1,0:T(8,128)(2,1)S(1)} %collective-permute-done.9, bf16[2,96,2560]{2,1,0:T(8,128)(2,1)S(1)} %collective-permute-done.8, ...), kind=kLoop, calls=%fused_computation.10 | loop fusion | flops 19660800 | bytes 7864320 | tf_op jit(solution)/shard_map/concatenate | solution.py:58
  148.7 2.9 pad_maximum_fusion
  152.1 6.1 %fusion.82 = (bf16[1152,768]{1,0:T(8,128)(2,1)}, f32[1152,768]{1,0:T(8,128)S(1)}) fusion(bf16[1152,2560]{1,0:T(8,128)(2,1)S(1)} %bitcast.123, bf16[768,2560]{1,0:T(8,128)(2,1)S(1)} %bitcast.129), kind=kOutput, calls=%fused_computation.155 | convolution fusion | flops 4530733056 | bytes 15138816 | tf_op jit(solution)/shard_map/dot_general | solution.py:105
  158.3 1.7 constant_dynamic-update-slice_fusion.1
  159.9 8.0 %fusion.81 = (bf16[1152,768]{1,0:T(8,128)(2,1)S(1)}, f32[1152,768]{1,0:T(8,128)S(1)}) fusion(bf16[1152,2560]{1,0:T(8,128)(2,1)} %bitcast.124, bf16[768,2560]{1,0:T(8,128)(2,1)} %bitcast.140), kind=kOutput, calls=%fused_computation.154 | convolution fusion | flops 4530733056 | bytes 15138816 | tf_op jit(solution)/shard_map/dot_general | solution.py:105
  170.2 1.8 convert_add_fusion
  174.4 4.5 %convolution_convert_fusion.2 = bf16[288,2560]{1,0:T(8,128)(2,1)} fusion(bf16[288,768]{1,0:T(8,128)(2,1)S(1)} %bitcast.139, bf16[768,2560]{1,0:T(8,128)(2,1)} %constant_dynamic-update-slice_fusion), kind=kOutput, calls=%fused_computation.4 | convolution fusion | flops 1133199360 | bytes 5849088 | tf_op jit(solution)/shard_map/dot_general | solution.py:123
  179.0 4.1 %all-to-all-start.3 = ((bf16[4,72,2560]{2,1,0:T(8,128)(2,1)}), bf16[4,72,2560]{2,1,0:T(8,128)(2,1)S(1)}, u32[]{:S(2)}, u32[]{:S(2)}) async-start(bf16[4,72,2560]{2,1,0:T(8,128)(2,1)} %bitcast.32), calls=%async_computation.3 | async-start | bytes 2949120 | tf_op jit(solution)/shard_map/all_to_all | solution.py:44
  183.1 4.6 %convolution_convert_fusion.1 = bf16[288,2560]{1,0:T(8,128)(2,1)} fusion(bf16[288,768]{1,0:T(8,128)(2,1)S(1)} %bitcast.138, bf16[768,2560]{1,0:T(8,128)(2,1)} %constant_dynamic-update-slice_fusion), kind=kOutput, calls=%fused_computation.3 | convolution fusion | flops 1133199360 | bytes 5849088 | tf_op jit(solution)/shard_map/dot_general | solution.py:123
  187.7 15.3 %all-to-all-done.3 = bf16[4,72,2560]{2,1,0:T(8,128)(2,1)S(1)} async-done(((bf16[4,72,2560]{2,1,0:T(8,128)(2,1)}), bf16[4,72,2560]{2,1,0:T(8,128)(2,1)S(1)}, u32[]{:S(2)}, u32[]{:S(2)}) %all-to-all-start.3) | async-done | bytes 1474592 | tf_op jit(solution)/shard_map/all_to_all | solution.py:44
  203.0 3.6 %all-to-all-start.4 = ((bf16[4,72,2560]{2,1,0:T(8,128)(2,1)}), bf16[4,72,2560]{2,1,0:T(8,128)(2,1)S(1)}, u32[]{:S(2)}, u32[]{:S(2)}) async-start(bf16[4,72,2560]{2,1,0:T(8,128)(2,1)} %bitcast.133), calls=%async_computation.4 | async-start | bytes 2949120 | tf_op jit(solution)/shard_map/all_to_all | solution.py:44
  206.7 4.7 %convolution_convert_fusion = bf16[288,2560]{1,0:T(8,128)(2,1)} fusion(bf16[288,768]{1,0:T(8,128)(2,1)} %bitcast.137, bf16[768,2560]{1,0:T(8,128)(2,1)} %constant_dynamic-update-slice_fusion), kind=kOutput, calls=%fused_computation.2 | convolution fusion | flops 1133199360 | bytes 5849088 | tf_op jit(solution)/shard_map/dot_general | solution.py:123
  211.4 14.1 %all-to-all-done.4 = bf16[4,72,2560]{2,1,0:T(8,128)(2,1)S(1)} async-done(((bf16[4,72,2560]{2,1,0:T(8,128)(2,1)}), bf16[4,72,2560]{2,1,0:T(8,128)(2,1)S(1)}, u32[]{:S(2)}, u32[]{:S(2)}) %all-to-all-start.4) | async-done | bytes 1474592 | tf_op jit(solution)/shard_map/all_to_all | solution.py:44
  225.5 4.3 %all-to-all-start.5 = ((bf16[4,72,2560]{2,1,0:T(8,128)(2,1)}), bf16[4,72,2560]{2,1,0:T(8,128)(2,1)}, u32[]{:S(2)}, u32[]{:S(2)}) async-start(bf16[4,72,2560]{2,1,0:T(8,128)(2,1)} %bitcast.134), calls=%async_computation.5 | async-start | bytes 2949120 | tf_op jit(solution)/shard_map/all_to_all | solution.py:44
  229.8 4.6 %convolution_convert_fusion.3 = bf16[288,2560]{1,0:T(8,128)(2,1)} fusion(bf16[288,768]{1,0:T(8,128)(2,1)S(1)} %bitcast.136, bf16[768,2560]{1,0:T(8,128)(2,1)} %constant_dynamic-update-slice_fusion), kind=kOutput, calls=%fused_computation.5 | convolution fusion | flops 1133199360 | bytes 5849088 | tf_op jit(solution)/shard_map/dot_general | solution.py:123
  236.5 21.8 %collective-permute-start.18 = (bf16[128,2560]{1,0:T(8,128)(2,1)}, bf16[128,2560]{1,0:T(8,128)(2,1)}, u32[]{:S(2)}, u32[]{:S(2)}) collective-permute-start(bf16[128,2560]{1,0:T(8,128)(2,1)} %fusion.7), channel_id=1, source_target_pairs={{0,144},{2,146},{4,148},{6,150},{8,24},{10,26},{12,28},{14,30},{16... | collective-permute-start | bytes 1966088 | tf_op jit(solution)/shard_map/ppermute | solution.py:40
  258.3 1.7 convolution_bitcast_fusion.2
  260.1 4.7 %all-to-all-start.2 = ((bf16[4,72,2560]{2,1,0:T(8,128)(2,1)}), bf16[4,72,2560]{2,1,0:T(8,128)(2,1)S(1)}, u32[]{:S(2)}, u32[]{:S(2)}) async-start(bf16[4,72,2560]{2,1,0:T(8,128)(2,1)} %bitcast.132), calls=%async_computation.2 | async-start | bytes 2949120 | tf_op jit(solution)/shard_map/all_to_all | solution.py:44
  264.8 2.8 fusion.6
  267.6 5.8 %collective-permute-start.19 = (bf16[128,2560]{1,0:T(8,128)(2,1)}, bf16[128,2560]{1,0:T(8,128)(2,1)}, u32[]{:S(2)}, u32[]{:S(2)}) collective-permute-start(bf16[128,2560]{1,0:T(8,128)(2,1)} %fusion.6), channel_id=1, source_target_pairs={{0,152},{2,154},{4,156},{6,158},{8,0},{10,2},{12,4},{14,6},{16,8},... | collective-permute-start | bytes 1966088 | tf_op jit(solution)/shard_map/ppermute | solution.py:32
  273.3 2.0 convolution_bitcast_fusion
  275.3 2.0 fusion.5
  277.4 4.9 %all-to-all-done.2 = bf16[4,72,2560]{2,1,0:T(8,128)(2,1)S(1)} async-done(((bf16[4,72,2560]{2,1,0:T(8,128)(2,1)}), bf16[4,72,2560]{2,1,0:T(8,128)(2,1)S(1)}, u32[]{:S(2)}, u32[]{:S(2)}) %all-to-all-start.2) | async-done | bytes 1474592 | tf_op jit(solution)/shard_map/all_to_all | solution.py:44
  282.9 2.2 collective-permute-done.19
  285.1 8.0 %collective-permute-done.20 = bf16[128,2560]{1,0:T(8,128)(2,1)} collective-permute-done((bf16[128,2560]{1,0:T(8,128)(2,1)S(1)}, bf16[128,2560]{1,0:T(8,128)(2,1)}, u32[]{:S(2)}, u32[]{:S(2)}) %collective-permute-start.20) | collective-permute-done | bytes 655392 | tf_op jit(solution)/shard_map/ppermute | solution.py:32
  293.1 3.2 %add_convert_fusion = bf16[128,2560]{1,0:T(8,128)(2,1)} fusion(bf16[128,2560]{1,0:T(8,128)(2,1)} %collective-permute-done.20, bf16[128,2560]{1,0:T(8,128)(2,1)} %collective-permute-done.19, bf16[128,2560]{1,0:T(8,128)(2,1)} %collective-permute-done.18, f32[128,2560]{1,0:T(8,128)S(1)} %convolution_bitcast_fusion.6, ...), kind=kOutput, calls=%fused_computation.40 | convolution fusion | flops 192131072 | bytes 6065952 | tf_op jit(solution)/shard_map/dot_general | solution.py:128
  (140 shorter events, 23.7 us)
Async XLA Ops:
  6.5 43.0 %copy-start.7 = (bf16[128,2560]{1,0:T(8,128)(2,1)S(1)}, bf16[128,2560]{1,0:T(8,128)(2,1)}, u32[]{:S(2)}) copy-start(bf16[128,2560]{1,0:T(8,128)(2,1)} %param.6) | copy-start | bytes 1966084
  6.5 40.5 %copy-start.6 = (bf16[1,2,96,2560]{3,2,1,0:T(8,128)(2,1)S(1)}, bf16[1,2,96,2560]{3,2,1,0:T(8,128)(2,1)}, u32[]{:S(2)}) copy-start(bf16[1,2,96,2560]{3,2,1,0:T(8,128)(2,1)} %param.10) | copy-start | bytes 2949124
  6.5 128.6 %all-gather.7.cloned.1.call-start = ((), (), s32[]{:S(2)}) async-start(), calls=%async_computation.7 | async-start | bytes 2457600 | tf_op jit(solution)/shard_map/all_gather | solution.py:90
  7.3 152.7 %all-gather.5.cloned.1.call-start = ((), (), s32[]{:S(2)}) async-start(), calls=%async_computation.6 | async-start | bytes 4915200 | tf_op jit(solution)/shard_map/all_gather | solution.py:89
  8.7 8.2 %collective-permute-start = (f32[128,12]{0,1:T(8,128)S(1)}, f32[128,12]{0,1:T(8,128)S(1)}, u32[]{:S(2)}, u32[]{:S(2)}) collective-permute-start(f32[128,12]{0,1:T(8,128)S(1)} %pad_maximum_fusion.3), channel_id=1, source_target_pairs={{0,8},{2,10},{4,12},{6,14},{8,16},{10,18},{12,20},{14,22},{16,24},... | collective-permute-start | bytes 18440 | tf_op jit(solution)/shard_map/ppermute | solution.py:32
  10.6 8.6 %collective-permute-start.2 = (f32[128,12]{0,1:T(8,128)S(1)}, f32[128,12]{0,1:T(8,128)S(1)}, u32[]{:S(2)}, u32[]{:S(2)}) collective-permute-start(f32[128,12]{0,1:T(8,128)S(1)} %pad_maximum_fusion.3), channel_id=1, source_target_pairs={{0,152},{2,154},{4,156},{6,158},{8,0},{10,2},{12,4},{14,6},{16,8},... | collective-permute-start | bytes 18440 | tf_op jit(solution)/shard_map/ppermute | solution.py:32
  10.7 9.1 %collective-permute-start.4 = (f32[128,12]{0,1:T(8,128)S(1)}, f32[128,12]{0,1:T(8,128)S(1)}, u32[]{:S(2)}, u32[]{:S(2)}) collective-permute-start(f32[128,12]{0,1:T(8,128)S(1)} %pad_maximum_fusion.3), channel_id=1, source_target_pairs={{0,16},{2,18},{4,20},{6,22},{8,152},{10,154},{12,156},{14,158},{16... | collective-permute-start | bytes 18440 | tf_op jit(solution)/shard_map/ppermute | solution.py:40
  16.4 17.9 %collective-permute-start.3 = (bf16[128,2560]{1,0:T(8,128)(2,1)}, bf16[128,2560]{1,0:T(8,128)(2,1)S(1)}, u32[]{:S(2)}, u32[]{:S(2)}) collective-permute-start(bf16[128,2560]{1,0:T(8,128)(2,1)} %param.6), channel_id=1, source_target_pairs={{0,152},{2,154},{4,156},{6,158},{8,0},{10,2},{12,4},{14,6},{16,8},... | collective-permute-start | bytes 1966088 | tf_op jit(solution)/shard_map/ppermute | solution.py:32
  16.4 39.2 %collective-permute-start.5 = (bf16[128,2560]{1,0:T(8,128)(2,1)}, bf16[128,2560]{1,0:T(8,128)(2,1)}, u32[]{:S(2)}, u32[]{:S(2)}) collective-permute-start(bf16[128,2560]{1,0:T(8,128)(2,1)} %param.6), channel_id=1, source_target_pairs={{0,16},{2,18},{4,20},{6,22},{8,152},{10,154},{12,156},{14,158},{16... | collective-permute-start | bytes 1966088 | tf_op jit(solution)/shard_map/ppermute | solution.py:40
  16.9 30.2 %collective-permute-start.1 = (bf16[128,2560]{1,0:T(8,128)(2,1)}, bf16[128,2560]{1,0:T(8,128)(2,1)S(1)}, u32[]{:S(2)}, u32[]{:S(2)}) collective-permute-start(bf16[128,2560]{1,0:T(8,128)(2,1)} %param.6), channel_id=1, source_target_pairs={{0,8},{2,10},{4,12},{6,14},{8,16},{10,18},{12,20},{14,22},{16,24},... | collective-permute-start | bytes 1966088 | tf_op jit(solution)/shard_map/ppermute | solution.py:32
  20.5 30.7 %copy-start.26 = (pred[128,4]{0,1:T(4,128)(4,1)}, pred[128,4]{0,1:T(4,128)(4,1)S(1)}, u32[]{:S(2)}) copy-start(pred[128,4]{0,1:T(4,128)(4,1)S(1)} %get-tuple-element.15) | copy-start | bytes 1540
  20.5 30.7 %copy-start.28 = (pred[128,4]{0,1:T(4,128)(4,1)}, pred[128,4]{0,1:T(4,128)(4,1)S(1)}, u32[]{:S(2)}) copy-start(pred[128,4]{0,1:T(4,128)(4,1)S(1)} %get-tuple-element.14) | copy-start | bytes 1540
  20.5 30.7 %copy-start.30 = (pred[128,4]{0,1:T(4,128)(4,1)}, pred[128,4]{0,1:T(4,128)(4,1)S(1)}, u32[]{:S(2)}) copy-start(pred[128,4]{0,1:T(4,128)(4,1)S(1)} %get-tuple-element.16) | copy-start | bytes 1540
  20.5 30.7 %copy-start.32 = (pred[128,4]{0,1:T(4,128)(4,1)}, pred[128,4]{0,1:T(4,128)(4,1)S(1)}, u32[]{:S(2)}) copy-start(pred[128,4]{0,1:T(4,128)(4,1)S(1)} %get-tuple-element.13) | copy-start | bytes 1540
  20.7 30.6 %copy-start.20 = (f32[128,4]{0,1:T(4,128)}, f32[128,4]{0,1:T(4,128)S(1)}, u32[]{:S(2)}) copy-start(f32[128,4]{0,1:T(4,128)S(1)} %fusion.57) | copy-start | bytes 6148
  20.8 30.4 %copy-start.16 = (f32[128,4]{0,1:T(4,128)}, f32[128,4]{0,1:T(4,128)S(1)}, u32[]{:S(2)}) copy-start(f32[128,4]{0,1:T(4,128)S(1)} %fusion.58) | copy-start | bytes 6148
  21.0 30.3 %copy-start.18 = (f32[128,4]{0,1:T(4,128)}, f32[128,4]{0,1:T(4,128)S(1)}, u32[]{:S(2)}) copy-start(f32[128,4]{0,1:T(4,128)S(1)} %fusion.59) | copy-start | bytes 6148
  21.2 30.1 %copy-start.14 = (f32[128,4]{0,1:T(4,128)}, f32[128,4]{0,1:T(4,128)S(1)}, u32[]{:S(2)}) copy-start(f32[128,4]{0,1:T(4,128)S(1)} %fusion.60) | copy-start | bytes 6148
  34.3 17.0 %copy-start.8 = (bf16[128,2560]{1,0:T(8,128)(2,1)}, bf16[128,2560]{1,0:T(8,128)(2,1)S(1)}, u32[]{:S(2)}) copy-start(bf16[128,2560]{1,0:T(8,128)(2,1)S(1)} %collective-permute-done.3) | copy-start | bytes 1966084
  47.1 40.8 %collective-permute-start.7 = (bf16[2,96,2560]{2,1,0:T(8,128)(2,1)S(1)}, bf16[2,96,2560]{2,1,0:T(8,128)(2,1)}, u32[]{:S(2)}, u32[]{:S(2)}) collective-permute-start(bf16[2,96,2560]{2,1,0:T(8,128)(2,1)S(1)} %bitcast.135), channel_id=1, source_target_pairs={{0,128},{2,130},{4,132},{6,134},{8,136},{10,138},{12,140},{14,142}... | collective-permute-start | bytes 2949128 | tf_op jit(solution)/shard_map/ppermute | solution.py:32
  51.3 42.1 %all-to-all-start = ((bf16[4,72,2560]{2,1,0:T(8,128)(2,1)}), bf16[4,72,2560]{2,1,0:T(8,128)(2,1)S(1)}, u32[]{:S(2)}, u32[]{:S(2)}) async-start(bf16[4,72,2560]{2,1,0:T(8,128)(2,1)} %bitcast.2), calls=%async_computation | async-start | bytes 2949120 | tf_op jit(solution)/shard_map/all_to_all | solution.py:44
  55.6 47.1 %collective-permute-start.13 = (bf16[96,2560]{1,0:T(8,128)(2,1)}, bf16[96,2560]{1,0:T(8,128)(2,1)}, u32[]{:S(2)}, u32[]{:S(2)}) collective-permute-start(bf16[96,2560]{1,0:T(8,128)(2,1)} %bitcast.27), channel_id=1, source_target_pairs={{0,128},{2,130},{4,132},{6,134},{8,136},{10,138},{12,140},{14,142}... | collective-permute-start | bytes 1474568 | tf_op jit(solution)/shard_map/ppermute | solution.py:32
  87.8 42.4 %collective-permute-start.8 = (bf16[2,96,2560]{2,1,0:T(8,128)(2,1)}, bf16[2,96,2560]{2,1,0:T(8,128)(2,1)S(1)}, u32[]{:S(2)}, u32[]{:S(2)}) collective-permute-start(bf16[2,96,2560]{2,1,0:T(8,128)(2,1)} %collective-permute-done.7), channel_id=1, source_target_pairs={{0,32},{2,34},{4,36},{6,38},{8,40},{10,42},{12,44},{14,46},{16,48}... | collective-permute-start | bytes 2949128 | tf_op jit(solution)/shard_map/ppermute | solution.py:32
  89.4 41.7 %collective-permute-start.9 = (bf16[2,96,2560]{2,1,0:T(8,128)(2,1)}, bf16[2,96,2560]{2,1,0:T(8,128)(2,1)S(1)}, u32[]{:S(2)}, u32[]{:S(2)}) collective-permute-start(bf16[2,96,2560]{2,1,0:T(8,128)(2,1)} %collective-permute-done.7), channel_id=1, source_target_pairs={{0,96},{2,98},{4,100},{6,102},{8,104},{10,106},{12,108},{14,110},{... | collective-permute-start | bytes 2949128 | tf_op jit(solution)/shard_map/ppermute | solution.py:32
  93.4 55.3 %all-to-all-start.1 = ((bf16[4,216,2560]{2,1,0:T(8,128)(2,1)}), bf16[4,216,2560]{2,1,0:T(8,128)(2,1)}, u32[]{:S(2)}, u32[]{:S(2)}) async-start(bf16[4,216,2560]{2,1,0:T(8,128)(2,1)} %bitcast.122), calls=%async_computation.1 | async-start | bytes 8847360 | tf_op jit(solution)/shard_map/all_to_all | solution.py:44
  102.8 22.7 %collective-permute-start.14 = (bf16[96,2560]{1,0:T(8,128)(2,1)}, bf16[96,2560]{1,0:T(8,128)(2,1)S(1)}, u32[]{:S(2)}, u32[]{:S(2)}) collective-permute-start(bf16[96,2560]{1,0:T(8,128)(2,1)} %collective-permute-done.13), channel_id=1, source_target_pairs={{0,32},{2,34},{4,36},{6,38},{8,40},{10,42},{12,44},{14,46},{16,48}... | collective-permute-start | bytes 1474568 | tf_op jit(solution)/shard_map/ppermute | solution.py:32
  104.4 21.9 %collective-permute-start.15 = (bf16[96,2560]{1,0:T(8,128)(2,1)}, bf16[96,2560]{1,0:T(8,128)(2,1)S(1)}, u32[]{:S(2)}, u32[]{:S(2)}) collective-permute-start(bf16[96,2560]{1,0:T(8,128)(2,1)} %collective-permute-done.13), channel_id=1, source_target_pairs={{0,96},{2,98},{4,100},{6,102},{8,104},{10,106},{12,108},{14,110},{... | collective-permute-start | bytes 1474568 | tf_op jit(solution)/shard_map/ppermute | solution.py:32
  126.3 32.0 %collective-permute-start.16 = (bf16[48,2560]{1,0:T(8,128)(2,1)}, bf16[48,2560]{1,0:T(8,128)(2,1)}, u32[]{:S(2)}, u32[]{:S(2)}) collective-permute-start(bf16[48,2560]{1,0:T(8,128)(2,1)} %slice.83), channel_id=1, source_target_pairs={{0,32},{2,34},{4,36},{6,38},{8,40},{10,42},{12,44},{14,46},{16,48}... | collective-permute-start | bytes 737288 | tf_op jit(solution)/shard_map/ppermute | solution.py:32
  127.1 41.4 %collective-permute-start.17 = (bf16[48,2560]{1,0:T(8,128)(2,1)}, bf16[48,2560]{1,0:T(8,128)(2,1)}, u32[]{:S(2)}, u32[]{:S(2)}) collective-permute-start(bf16[48,2560]{1,0:T(8,128)(2,1)} %slice.84), channel_id=1, source_target_pairs={{0,96},{2,98},{4,100},{6,102},{8,104},{10,106},{12,108},{14,110},{... | collective-permute-start | bytes 737288 | tf_op jit(solution)/shard_map/ppermute | solution.py:32
  131.1 14.2 %collective-permute-start.10 = (bf16[1,96,2560]{2,1,0:T(8,128)(2,1)}, bf16[1,96,2560]{2,1,0:T(8,128)(2,1)}, u32[]{:S(2)}, u32[]{:S(2)}) collective-permute-start(bf16[1,96,2560]{2,1,0:T(8,128)(2,1)} %slice.77), channel_id=1, source_target_pairs={{0,32},{2,34},{4,36},{6,38},{8,40},{10,42},{12,44},{14,46},{16,48}... | collective-permute-start | bytes 1474568 | tf_op jit(solution)/shard_map/ppermute | solution.py:32
  131.9 13.4 %collective-permute-start.11 = (bf16[1,96,2560]{2,1,0:T(8,128)(2,1)}, bf16[1,96,2560]{2,1,0:T(8,128)(2,1)}, u32[]{:S(2)}, u32[]{:S(2)}) collective-permute-start(bf16[1,96,2560]{2,1,0:T(8,128)(2,1)} %slice.78), channel_id=1, source_target_pairs={{0,96},{2,98},{4,100},{6,102},{8,104},{10,106},{12,108},{14,110},{... | collective-permute-start | bytes 1474568 | tf_op jit(solution)/shard_map/ppermute | solution.py:32
  158.2 11.9 %collective-permute-start.12 = (bf16[1152,768]{1,0:T(8,128)(2,1)}, bf16[1152,768]{1,0:T(8,128)(2,1)}, u32[]{:S(2)}, u32[]{:S(2)}) collective-permute-start(bf16[1152,768]{1,0:T(8,128)(2,1)} %get-tuple-element.43), channel_id=1, source_target_pairs={{0,1},{1,0},{2,3},{3,2},{4,5},{5,4},{6,7},{7,6},{8,9},{9,8},{10,11... | collective-permute-start | bytes 5308424 | tf_op jit(solution)/shard_map/ppermute | solution.py:111
  167.9 4.6 %collective-permute-start.6 = (bf16[1152,768]{1,0:T(8,128)(2,1)S(1)}, bf16[1152,768]{1,0:T(8,128)(2,1)S(1)}, u32[]{:S(2)}, u32[]{:S(2)}) collective-permute-start(bf16[1152,768]{1,0:T(8,128)(2,1)S(1)} %get-tuple-element.41), channel_id=1, source_target_pairs={{0,1},{1,0},{2,3},{3,2},{4,5},{5,4},{6,7},{7,6},{8,9},{9,8},{10,11... | collective-permute-start | bytes 5308424 | tf_op jit(solution)/shard_map/ppermute | solution.py:111
  179.0 24.0 %all-to-all-start.3 = ((bf16[4,72,2560]{2,1,0:T(8,128)(2,1)}), bf16[4,72,2560]{2,1,0:T(8,128)(2,1)S(1)}, u32[]{:S(2)}, u32[]{:S(2)}) async-start(bf16[4,72,2560]{2,1,0:T(8,128)(2,1)} %bitcast.32), calls=%async_computation.3 | async-start | bytes 2949120 | tf_op jit(solution)/shard_map/all_to_all | solution.py:44
  187.7 18.9 %copy-start.13 = (s32[128,6]{0,1:T(8,128)S(1)}, s32[128,6]{0,1:T(8,128)}, u32[]{:S(2)}) copy-start(s32[128,6]{0,1:T(8,128)} %copy-done.12) | copy-start | bytes 9220
  187.7 18.9 %copy-start.22 = (f32[128,6]{0,1:T(8,128)S(1)}, f32[128,6]{0,1:T(8,128)}, u32[]{:S(2)}) copy-start(f32[128,6]{0,1:T(8,128)} %param.9) | copy-start | bytes 9220
  187.7 18.9 %copy-start.23 = (f32[128,6]{0,1:T(8,128)S(1)}, f32[128,6]{0,1:T(8,128)}, u32[]{:S(2)}) copy-start(f32[128,6]{0,1:T(8,128)} %get-tuple-element.21) | copy-start | bytes 9220
  187.7 18.9 %copy-start.24 = (f32[128,6]{0,1:T(8,128)S(1)}, f32[128,6]{0,1:T(8,128)}, u32[]{:S(2)}) copy-start(f32[128,6]{0,1:T(8,128)} %get-tuple-element.23) | copy-start | bytes 9220
  187.7 18.9 %copy-start.25 = (f32[128,6]{0,1:T(8,128)S(1)}, f32[128,6]{0,1:T(8,128)}, u32[]{:S(2)}) copy-start(f32[128,6]{0,1:T(8,128)} %get-tuple-element.25) | copy-start | bytes 9220
  187.7 18.9 %copy-start.35 = (s32[4]{0:T(128)S(1)}, s32[4]{0:T(128)}, u32[]{:S(2)}) copy-start(s32[4]{0:T(128)} %copy-done.34) | copy-start | bytes 52
  203.0 22.5 %all-to-all-start.4 = ((bf16[4,72,2560]{2,1,0:T(8,128)(2,1)}), bf16[4,72,2560]{2,1,0:T(8,128)(2,1)S(1)}, u32[]{:S(2)}, u32[]{:S(2)}) async-start(bf16[4,72,2560]{2,1,0:T(8,128)(2,1)} %bitcast.133), calls=%async_computation.4 | async-start | bytes 2949120 | tf_op jit(solution)/shard_map/all_to_all | solution.py:44
  225.5 34.6 %all-to-all-start.5 = ((bf16[4,72,2560]{2,1,0:T(8,128)(2,1)}), bf16[4,72,2560]{2,1,0:T(8,128)(2,1)}, u32[]{:S(2)}, u32[]{:S(2)}) async-start(bf16[4,72,2560]{2,1,0:T(8,128)(2,1)} %bitcast.134), calls=%async_computation.5 | async-start | bytes 2949120 | tf_op jit(solution)/shard_map/all_to_all | solution.py:44
  235.0 23.3 %copy-start.19 = (f32[128,4]{0,1:T(4,128)S(1)}, f32[128,4]{0,1:T(4,128)}, u32[]{:S(2)}) copy-start(f32[128,4]{0,1:T(4,128)} %copy-done.18) | copy-start | bytes 6148
  235.0 23.3 %copy-start.29 = (pred[128,4]{0,1:T(4,128)(4,1)S(1)}, pred[128,4]{0,1:T(4,128)(4,1)}, u32[]{:S(2)}) copy-start(pred[128,4]{0,1:T(4,128)(4,1)} %copy-done.28) | copy-start | bytes 1540
  236.5 46.4 %collective-permute-start.18 = (bf16[128,2560]{1,0:T(8,128)(2,1)}, bf16[128,2560]{1,0:T(8,128)(2,1)}, u32[]{:S(2)}, u32[]{:S(2)}) collective-permute-start(bf16[128,2560]{1,0:T(8,128)(2,1)} %fusion.7), channel_id=1, source_target_pairs={{0,144},{2,146},{4,148},{6,150},{8,24},{10,26},{12,28},{14,30},{16... | collective-permute-start | bytes 1966088 | tf_op jit(solution)/shard_map/ppermute | solution.py:40
  260.1 22.2 %all-to-all-start.2 = ((bf16[4,72,2560]{2,1,0:T(8,128)(2,1)}), bf16[4,72,2560]{2,1,0:T(8,128)(2,1)S(1)}, u32[]{:S(2)}, u32[]{:S(2)}) async-start(bf16[4,72,2560]{2,1,0:T(8,128)(2,1)} %bitcast.132), calls=%async_computation.2 | async-start | bytes 2949120 | tf_op jit(solution)/shard_map/all_to_all | solution.py:44
  267.6 17.6 %collective-permute-start.19 = (bf16[128,2560]{1,0:T(8,128)(2,1)}, bf16[128,2560]{1,0:T(8,128)(2,1)}, u32[]{:S(2)}, u32[]{:S(2)}) collective-permute-start(bf16[128,2560]{1,0:T(8,128)(2,1)} %fusion.6), channel_id=1, source_target_pairs={{0,152},{2,154},{4,156},{6,158},{8,0},{10,2},{12,4},{14,6},{16,8},... | collective-permute-start | bytes 1966088 | tf_op jit(solution)/shard_map/ppermute | solution.py:32
  277.3 15.8 %collective-permute-start.20 = (bf16[128,2560]{1,0:T(8,128)(2,1)S(1)}, bf16[128,2560]{1,0:T(8,128)(2,1)}, u32[]{:S(2)}, u32[]{:S(2)}) collective-permute-start(bf16[128,2560]{1,0:T(8,128)(2,1)S(1)} %fusion.5), channel_id=1, source_target_pairs={{0,8},{2,10},{4,12},{6,14},{8,16},{10,18},{12,20},{14,22},{16,24},... | collective-permute-start | bytes 1966088 | tf_op jit(solution)/shard_map/ppermute | solution.py:32
  (17 other events, 91.9 us)
Sparse Core Ops, SparseCore 0:
  9.2 34.5 all-gather.6
  45.6 52.1 all-gather.4
